TPU v7x, 32 devices: a whole 2x2x4 slice. The times are simulated.
32 devices in a mesh: ctx: 16 (over z, y, core), ch: 2 (over x).
Axes of the slice: x: 2, y: 2, z: 4, core: 2. Of those that a mesh axis runs over, the one named last changes fastest.
Arguments:
- inputs: bfloat16 [2048, 4096], P('ctx', 'ch'), may hold values from -0.125 to 0.125
- out_grad: bfloat16 [2048, 4096], P('ctx', 'ch'), may hold values from -6 to 6
- filter_taps: bfloat16 [512, 4096], P('ctx', 'ch'), may hold values from -0.25 to 0.25
- skip_gain: float32 [4096], P('ch'), may hold values from 0.3 to 3
Outputs:
- input_grad: float32 [2048, 4096], P('ctx', 'ch')
- filter_grad: float32 [512, 4096], P('ctx', 'ch')
All inputs are finite; a program needn't handle non-finite values.
Results may differ from a plain program's by a relative error of at most 0.0003.
Values may be sent and summed in bfloat16 or wider, within the bound.
A program may use at most 128 MiB of HBM per device.

v0:
```python
import math

import jax
import jax.numpy as jnp
from jax import lax
from jax.sharding import PartitionSpec as P

FBLOCKS = 4


def passed_along(array, axis, by):
    length = lax.axis_size(axis)
    pairs = [(i, i + by) for i in range(length) if 0 <= i + by < length]
    return lax.ppermute(array, axis, pairs)


def forward_table(length):
    window = 2 * length
    freqs = jnp.arange(length + 1, dtype=jnp.int32)[:, None]
    places = jnp.arange(length, dtype=jnp.int32)[None, :]
    angle = 2.0 * math.pi / window * (freqs * places % window).astype(jnp.float32)
    return jnp.concatenate([jnp.cos(angle), -jnp.sin(angle)], axis=0)


def inverse_table(length):
    window = 2 * length
    samples = jnp.arange(window, dtype=jnp.int32)[:, None]
    freqs = jnp.arange(length + 1, dtype=jnp.int32)[None, :]
    angle = 2.0 * math.pi / window * (samples * freqs % window).astype(jnp.float32)
    edges = jnp.logical_or(freqs == 0, freqs == length)
    weights = jnp.where(edges, 1.0, 2.0).astype(jnp.float32)
    return jnp.concatenate([weights * jnp.cos(angle), -weights * jnp.sin(angle)], axis=1) / window


def spectrum(table, block):
    return jnp.dot(table, block.astype(jnp.float32), precision=lax.Precision.HIGHEST)


def times_conj(first, second):
    middle = first.shape[0] // 2
    first_real, first_imag = (first[:middle], first[middle:])
    second_real, second_imag = (second[:middle], second[middle:])
    return jnp.concatenate(
        [
            first_real * second_real + first_imag * second_imag,
            first_imag * second_real - first_real * second_imag,
        ],
        axis=0,
    )


def incoming_inputs(inputs, own, table):
    arrivals = [own]
    current = inputs
    for offset in range(FBLOCKS):
        current = passed_along(current, "ctx", 1)
        arrivals.append(spectrum(table, current))
    return arrivals


def incoming_grads(out_grad, own, table):
    arrivals = [own]
    current = out_grad
    for offset in range(FBLOCKS):
        current = passed_along(current, "ctx", -1)
        arrivals.append(spectrum(table, current))
    return arrivals


def body(inputs, out_grad, filter_taps, skip_gain):
    length = inputs.shape[0]
    table = forward_table(length)
    inverse = inverse_table(length)
    gathered = lax.all_gather(filter_taps, "ctx", axis=0, tiled=True)
    columns = gathered.shape[1]
    filter_rows = gathered.astype(jnp.float32).reshape(FBLOCKS, length, columns)
    pieces = jnp.einsum("fr,mrc->mfc", table, filter_rows, precision=lax.Precision.HIGHEST)
    oddness = (jnp.arange(length + 1, dtype=jnp.int32) % 2).astype(jnp.float32)
    parity = jnp.tile(1.0 - 2.0 * oddness, 2)
    empty = jnp.zeros((1, 2 * (length + 1), columns), jnp.float32)
    windows = jnp.concatenate([pieces, empty], axis=0) + parity[None, :, None] * jnp.concatenate(
        [empty, pieces], axis=0
    )
    own_inputs = spectrum(table, inputs)
    own_grads = spectrum(table, out_grad)
    input_list = incoming_inputs(inputs, own_inputs, table)
    grad_list = incoming_grads(out_grad, own_grads, table)
    combined = times_conj(grad_list[0], windows[0])
    for offset in range(1, FBLOCKS + 1):
        combined = combined + times_conj(grad_list[offset], windows[offset])
    conv_part = jnp.dot(inverse[:length], combined, precision=lax.Precision.HIGHEST)
    input_grad = skip_gain[None, :] * out_grad.astype(jnp.float32) + conv_part
    products = jnp.stack([times_conj(own_grads, arrived) for arrived in input_list])
    lags = jnp.einsum("if,mfc->mic", inverse, products, precision=lax.Precision.HIGHEST)
    tap_terms = (lags[:FBLOCKS, :length] + lags[1:, length:]).reshape(FBLOCKS * length, columns)
    filter_grad = lax.psum_scatter(tap_terms, "ctx", scatter_dimension=0, tiled=True)
    return (input_grad, filter_grad)


def solution(mesh):
    in_specs = (P("ctx", "ch"), P("ctx", "ch"), P("ctx", "ch"), P("ch"))
    out_specs = (P("ctx", "ch"), P("ctx", "ch"))
    return jax.shard_map(body, mesh=mesh, in_specs=in_specs, out_specs=out_specs, check_vma=False)
```

profile of v0, /device:TPU:1, one launch (start us, length us, event | category | flops | bytes accessed | tf_op | source)
XLA Modules:
  0.0 213.0 jit_solution(9094990899509313575)
XLA Ops:
  7.2 0.0 copy-start.8
  7.2 0.0 all-gather.2.cloned.1.call-start
  7.2 4.7 %collective-permute-start.4 = (bf16[128,2048]{1,0:T(8,128)(2,1)}, bf16[128,2048]{1,0:T(8,128)(2,1)S(1)}, u32[]{:S(2)}, u32[]{:S(2)}) collective-permute-start(bf16[128,2048]{1,0:T(8,128)(2,1)} %param.4), channel_id=1, source_target_pairs={{0,2},{2,4},{4,6},{6,8},{8,10},{10,12},{12,14},{14,16},{16,18},{18... | collective-permute-start | bytes 1572872 | tf_op jit(solution)/shard_map/ppermute | solution.py:14
  11.9 0.0 all-gather.2.cloned.1.call-update
  11.9 0.0 reduce-scatter.2.cloned.1.call-start
  12.0 0.1 mul.233
  12.1 0.3 sine_negate_fusion
  12.4 0.6 sine_multiply_fusion
  13.0 0.7 maximum_multiply_fusion
  13.7 4.6 %collective-permute-done.4 = bf16[128,2048]{1,0:T(8,128)(2,1)S(1)} collective-permute-done((bf16[128,2048]{1,0:T(8,128)(2,1)}, bf16[128,2048]{1,0:T(8,128)(2,1)S(1)}, u32[]{:S(2)}, u32[]{:S(2)}) %collective-permute-start.4) | collective-permute-done | bytes 524320 | tf_op jit(solution)/shard_map/ppermute | solution.py:14
  18.3 4.3 %collective-permute-start.5 = (bf16[128,2048]{1,0:T(8,128)(2,1)S(1)}, bf16[128,2048]{1,0:T(8,128)(2,1)S(1)}, u32[]{:S(2)}, u32[]{:S(2)}) collective-permute-start(bf16[128,2048]{1,0:T(8,128)(2,1)S(1)} %collective-permute-done.4), channel_id=1, source_target_pairs={{0,2},{2,4},{4,6},{6,8},{8,10},{10,12},{12,14},{14,16},{16,18},{18... | collective-permute-start | bytes 1572872 | tf_op jit(solution)/shard_map/ppermute | solution.py:14
  22.6 0.0 copy-done.8
  22.6 0.0 copy-start.5
  22.6 1.0 fusion.48
  23.6 0.0 copy-done.5
  23.6 1.0 fusion.53
  24.6 4.0 %collective-permute-done.5 = bf16[128,2048]{1,0:T(8,128)(2,1)S(1)} collective-permute-done((bf16[128,2048]{1,0:T(8,128)(2,1)S(1)}, bf16[128,2048]{1,0:T(8,128)(2,1)S(1)}, u32[]{:S(2)}, u32[]{:S(2)}) %collective-permute-start.5) | collective-permute-done | bytes 524320 | tf_op jit(solution)/shard_map/ppermute | solution.py:14
  28.7 4.4 %collective-permute-start.6 = (bf16[128,2048]{1,0:T(8,128)(2,1)S(1)}, bf16[128,2048]{1,0:T(8,128)(2,1)S(1)}, u32[]{:S(2)}, u32[]{:S(2)}) collective-permute-start(bf16[128,2048]{1,0:T(8,128)(2,1)S(1)} %collective-permute-done.5), channel_id=1, source_target_pairs={{0,2},{2,4},{4,6},{6,8},{8,10},{10,12},{12,14},{14,16},{16,18},{18... | collective-permute-start | bytes 1572872 | tf_op jit(solution)/shard_map/ppermute | solution.py:14
  33.1 1.0 fusion.47
  34.1 2.3 %fusion.46 = f32[258,2048]{1,0:T(8,128)} fusion(bf16[128,2048]{1,0:T(8,128)(2,1)S(1)} %collective-permute-done.5, f32[129,128]{1,0:T(8,128)S(1)} %get-tuple-element.32, f32[129,128]{1,0:T(8,128)S(1)} %get-tuple-element.33), kind=kOutput, calls=%fused_computation.99 | convolution fusion | flops 811630848 | bytes 2769920 | tf_op jit(solution)/shard_map/dot_general | solution.py:36
  36.4 5.9 %collective-permute-done.6 = bf16[128,2048]{1,0:T(8,128)(2,1)S(1)} collective-permute-done((bf16[128,2048]{1,0:T(8,128)(2,1)S(1)}, bf16[128,2048]{1,0:T(8,128)(2,1)S(1)}, u32[]{:S(2)}, u32[]{:S(2)}) %collective-permute-start.6) | collective-permute-done | bytes 524320 | tf_op jit(solution)/shard_map/ppermute | solution.py:14
  42.3 4.4 %collective-permute-start.7 = (bf16[128,2048]{1,0:T(8,128)(2,1)S(1)}, bf16[128,2048]{1,0:T(8,128)(2,1)S(1)}, u32[]{:S(2)}, u32[]{:S(2)}) collective-permute-start(bf16[128,2048]{1,0:T(8,128)(2,1)S(1)} %collective-permute-done.6), channel_id=1, source_target_pairs={{0,2},{2,4},{4,6},{6,8},{8,10},{10,12},{12,14},{14,16},{16,18},{18... | collective-permute-start | bytes 1572872 | tf_op jit(solution)/shard_map/ppermute | solution.py:14
  46.7 1.0 fusion.45
  47.7 2.1 multiply_add_fusion.2
  49.8 3.0 %collective-permute-done.7 = bf16[128,2048]{1,0:T(8,128)(2,1)S(1)} collective-permute-done((bf16[128,2048]{1,0:T(8,128)(2,1)S(1)}, bf16[128,2048]{1,0:T(8,128)(2,1)S(1)}, u32[]{:S(2)}, u32[]{:S(2)}) %collective-permute-start.7) | collective-permute-done | bytes 524320 | tf_op jit(solution)/shard_map/ppermute | solution.py:14
  52.8 1.0 fusion.44
  53.8 2.1 multiply_add_fusion.1
  55.9 1.6 fusion.18
  57.5 1.5 fusion.19
  59.0 7.4 %convolution_bitcast_fusion.1 = f32[4,258,2048]{2,1,0:T(8,128)} fusion(bf16[4,128,2048]{2,1,0:T(8,128)(2,1)} %bitcast.105, f32[129,128]{1,0:T(8,128)S(1)} %get-tuple-element.32, f32[129,128]{1,0:T(8,128)S(1)} %get-tuple-element.33), kind=kOutput, calls=%fused_computation.2 | convolution fusion | flops 3246424320 | bytes 10683392 | tf_op jit(solution)/shard_map/fr,mrc->mfc/dot_general | solution.py:77
  66.4 13.6 %multiply_add_fusion = f32[5,258,2048]{2,1,0:T(8,128)} fusion(f32[4,258,2048]{2,1,0:T(8,128)} %convolution_bitcast_fusion.1, f32[258]{0:T(512)S(1)} %mul.233), kind=kLoop, calls=%fused_computation | loop fusion | flops 5283840 | bytes 19022856 | tf_op jit(solution)/shard_map/add | solution.py:81
  80.0 4.1 %multiply_add_fusion.3 = (f32[129,2048]{1,0:T(8,128)S(1)}, f32[129,2048]{1,0:T(8,128)S(1)}, f32[129,2048]{1,0:T(8,128)S(1)}, f32[129,2048]{1,0:T(8,128)}) fusion(f32[258,2048]{1,0:T(8,128)} %fusion.46, f32[258,2048]{1,0:T(8,128)S(1)} %fusion.53, f32[5,258,2048]{2,1,0:T(8,128)} %multiply_add_fusion), kind=kLoop, calls=%fused_computation.48 | loop fusion | flops 3170304 | bytes 10567680 | tf_op jit(solution)/shard_map/add | solution.py:45
  84.1 1.5 fusion.20
  85.6 0.1 copy-done.1
  85.7 0.8 copy-done.2
  86.5 1.5 fusion.21
  88.0 0.0 copy-done.3
  88.1 0.8 copy-done.4
  88.9 1.5 fusion.22
  90.4 0.0 copy-done.7
  90.4 23.8 %convolution_bitcast_fusion = f32[5,256,2048]{2,1,0:T(8,128)S(1)} fusion(f32[5,258,2048]{2,1,0:T(8,128)} %fusion.22, f32[256,258]{0,1:T(8,128)S(1)} %copy-done.7), kind=kOutput, calls=%fused_computation.1 | convolution fusion | flops 8115978240 | bytes 21317632 | tf_op jit(solution)/shard_map/if,mfc->mic/dot_general | solution.py:94
  114.2 2.8 %slice_add_fusion = f32[4,128,2048]{2,1,0:T(8,128)} fusion(f32[5,256,2048]{2,1,0:T(8,128)S(1)} %convolution_bitcast_fusion), kind=kLoop, calls=%fused_computation.3 | loop fusion | flops 1048576 | bytes 12582912 | tf_op jit(solution)/shard_map/add | solution.py:95
  117.0 0.0 reduce-scatter.2.cloned.1.call-update
  117.1 1.0 copy-done.6
  118.1 1.9 collective-permute-start
  120.0 12.4 %collective-permute-done = bf16[128,2048]{1,0:T(8,128)(2,1)S(1)} collective-permute-done((bf16[128,2048]{1,0:T(8,128)(2,1)S(1)}, bf16[128,2048]{1,0:T(8,128)(2,1)S(1)}, u32[]{:S(2)}, u32[]{:S(2)}) %collective-permute-start) | collective-permute-done | bytes 524320 | tf_op jit(solution)/shard_map/ppermute | solution.py:14
  132.4 1.9 collective-permute-start.1
  134.3 8.6 %collective-permute-done.1 = bf16[128,2048]{1,0:T(8,128)(2,1)S(1)} collective-permute-done((bf16[128,2048]{1,0:T(8,128)(2,1)S(1)}, bf16[128,2048]{1,0:T(8,128)(2,1)S(1)}, u32[]{:S(2)}, u32[]{:S(2)}) %collective-permute-start.1) | collective-permute-done | bytes 524320 | tf_op jit(solution)/shard_map/ppermute | solution.py:14
  142.9 2.1 collective-permute-start.2
  145.1 1.0 fusion.52
  146.1 8.2 %collective-permute-done.2 = bf16[128,2048]{1,0:T(8,128)(2,1)S(1)} collective-permute-done((bf16[128,2048]{1,0:T(8,128)(2,1)S(1)}, bf16[128,2048]{1,0:T(8,128)(2,1)S(1)}, u32[]{:S(2)}, u32[]{:S(2)}) %collective-permute-start.2) | collective-permute-done | bytes 524320 | tf_op jit(solution)/shard_map/ppermute | solution.py:14
  154.2 1.9 collective-permute-start.3
  156.2 1.0 fusion.51
  157.2 1.0 fusion.50
  158.2 16.7 %collective-permute-done.3 = bf16[128,2048]{1,0:T(8,128)(2,1)S(1)} collective-permute-done((bf16[128,2048]{1,0:T(8,128)(2,1)S(1)}, bf16[128,2048]{1,0:T(8,128)(2,1)S(1)}, u32[]{:S(2)}, u32[]{:S(2)}) %collective-permute-start.3) | collective-permute-done | bytes 524320 | tf_op jit(solution)/shard_map/ppermute | solution.py:14
  174.8 1.0 fusion.49
  175.8 3.3 %multiply_add_fusion.8 = (f32[129,2048]{1,0:T(8,128)S(1)}, f32[129,2048]{1,0:T(8,128)S(1)}, f32[129,2048]{1,0:T(8,128)S(1)}, f32[129,2048]{1,0:T(8,128)S(1)}) fusion(f32[5,258,2048]{2,1,0:T(8,128)} %multiply_add_fusion, f32[258,2048]{1,0:T(8,128)S(1)} %fusion.51, f32[258,2048]{1,0:T(8,128)S(1)} %fusion.52), kind=kLoop, calls=%fused_computation.58 | loop fusion | flops 3170304 | bytes 12681216 | tf_op jit(solution)/shard_map/add | solution.py:45
  179.2 0.0 copy-start
  179.2 0.0 copy-start.9
  179.2 3.5 %multiply_add_fusion.6 = (f32[129,2048]{1,0:T(8,128)S(1)}, f32[129,2048]{1,0:T(8,128)S(1)}, f32[129,2048]{1,0:T(8,128)S(1)}, f32[129,2048]{1,0:T(8,128)S(1)}) fusion(f32[5,258,2048]{2,1,0:T(8,128)} %multiply_add_fusion, f32[258,2048]{1,0:T(8,128)S(1)} %fusion.49, f32[258,2048]{1,0:T(8,128)S(1)} %fusion.50), kind=kLoop, calls=%fused_computation.54 | loop fusion | flops 3170304 | bytes 12681216 | tf_op jit(solution)/shard_map/add | solution.py:45
  182.7 0.0 copy-done
  182.7 0.0 copy-done.9
  182.7 3.8 %convolution_add_fusion = f32[128,2048]{1,0:T(8,128)} fusion(f32[129,2048]{1,0:T(8,128)S(1)} %get-tuple-element.30, f32[129,2048]{1,0:T(8,128)S(1)} %copy-done, f32[129,2048]{1,0:T(8,128)S(1)} %get-tuple-element.14, f32[129,2048]{1,0:T(8,128)S(1)} %get-tuple-element.15, f32[129,2048]{1,0:T(8,128)S(1)} %get-tuple-element.7, ...), kind=kOutput, calls=%fused_computation.4 | convolution fusion | flops 817139712 | bytes 12857344 | tf_op jit(solution)/shard_map/dot_general | solution.py:91
  186.6 19.6 %reduce-scatter.2.cloned.1.call-done = f32[32,2048]{1,0:T(8,128)} async-done(((f32[512,2048]{1,0:T(8,128)}), f32[32,2048]{1,0:T(8,128)}) %reduce-scatter.2.cloned.1.call-update) | async-done | bytes 262160 | tf_op jit(solution)/shard_map/reduce_scatter | solution.py:96
  (11 shorter events, 0.0 us)
Async XLA Ops:
  7.2 15.4 %copy-start.8 = (bf16[128,2048]{1,0:T(8,128)(2,1)S(1)}, bf16[128,2048]{1,0:T(8,128)(2,1)}, u32[]{:S(2)}) copy-start(bf16[128,2048]{1,0:T(8,128)(2,1)} %param.4) | copy-start | bytes 1572868
  7.2 51.8 %all-gather.2.cloned.1.call-start = ((), (), s32[]{:S(2)}) async-start(), calls=%async_computation.1 | async-start | bytes 2228224 | tf_op jit(solution)/shard_map/all_gather | solution.py:74
  7.2 11.1 %collective-permute-start.4 = (bf16[128,2048]{1,0:T(8,128)(2,1)}, bf16[128,2048]{1,0:T(8,128)(2,1)S(1)}, u32[]{:S(2)}, u32[]{:S(2)}) collective-permute-start(bf16[128,2048]{1,0:T(8,128)(2,1)} %param.4), channel_id=1, source_target_pairs={{0,2},{2,4},{4,6},{6,8},{8,10},{10,12},{12,14},{14,16},{16,18},{18... | collective-permute-start | bytes 1572872 | tf_op jit(solution)/shard_map/ppermute | solution.py:14
  11.9 194.2 %reduce-scatter.2.cloned.1.call-start = ((), (), s32[]{:S(2)}) async-start(), calls=%async_computation.2 | async-start | bytes 4456448 | tf_op jit(solution)/shard_map/reduce_scatter | solution.py:96
  18.3 10.4 %collective-permute-start.5 = (bf16[128,2048]{1,0:T(8,128)(2,1)S(1)}, bf16[128,2048]{1,0:T(8,128)(2,1)S(1)}, u32[]{:S(2)}, u32[]{:S(2)}) collective-permute-start(bf16[128,2048]{1,0:T(8,128)(2,1)S(1)} %collective-permute-done.4), channel_id=1, source_target_pairs={{0,2},{2,4},{4,6},{6,8},{8,10},{10,12},{12,14},{14,16},{16,18},{18... | collective-permute-start | bytes 1572872 | tf_op jit(solution)/shard_map/ppermute | solution.py:14
  22.6 1.0 copy-start.5
  28.7 13.6 %collective-permute-start.6 = (bf16[128,2048]{1,0:T(8,128)(2,1)S(1)}, bf16[128,2048]{1,0:T(8,128)(2,1)S(1)}, u32[]{:S(2)}, u32[]{:S(2)}) collective-permute-start(bf16[128,2048]{1,0:T(8,128)(2,1)S(1)} %collective-permute-done.5), channel_id=1, source_target_pairs={{0,2},{2,4},{4,6},{6,8},{8,10},{10,12},{12,14},{14,16},{16,18},{18... | collective-permute-start | bytes 1572872 | tf_op jit(solution)/shard_map/ppermute | solution.py:14
  42.3 10.5 %collective-permute-start.7 = (bf16[128,2048]{1,0:T(8,128)(2,1)S(1)}, bf16[128,2048]{1,0:T(8,128)(2,1)S(1)}, u32[]{:S(2)}, u32[]{:S(2)}) collective-permute-start(bf16[128,2048]{1,0:T(8,128)(2,1)S(1)} %collective-permute-done.6), channel_id=1, source_target_pairs={{0,2},{2,4},{4,6},{6,8},{8,10},{10,12},{12,14},{14,16},{16,18},{18... | collective-permute-start | bytes 1572872 | tf_op jit(solution)/shard_map/ppermute | solution.py:14
  84.1 1.6 copy-start.1
  84.1 2.4 %copy-start.2 = (f32[129,2048]{1,0:T(8,128)S(1)}, f32[129,2048]{1,0:T(8,128)}, u32[]{:S(2)}) copy-start(f32[129,2048]{1,0:T(8,128)} %get-tuple-element.19) | copy-start | bytes 3170308
  86.5 1.6 copy-start.3
  86.5 2.4 %copy-start.4 = (f32[129,2048]{1,0:T(8,128)S(1)}, f32[129,2048]{1,0:T(8,128)}, u32[]{:S(2)}) copy-start(f32[129,2048]{1,0:T(8,128)} %get-tuple-element.17) | copy-start | bytes 3170308
  88.9 1.6 copy-start.7
  117.0 1.0 copy-start.6
  118.1 14.3 %collective-permute-start = (bf16[128,2048]{1,0:T(8,128)(2,1)S(1)}, bf16[128,2048]{1,0:T(8,128)(2,1)S(1)}, u32[]{:S(2)}, u32[]{:S(2)}) collective-permute-start(bf16[128,2048]{1,0:T(8,128)(2,1)S(1)} %copy-done.6), channel_id=1, source_target_pairs={{2,0},{4,2},{6,4},{8,6},{10,8},{12,10},{14,12},{16,14},{18,16},{20... | collective-permute-start | bytes 1572872 | tf_op jit(solution)/shard_map/ppermute | solution.py:14
  132.4 10.5 %collective-permute-start.1 = (bf16[128,2048]{1,0:T(8,128)(2,1)S(1)}, bf16[128,2048]{1,0:T(8,128)(2,1)S(1)}, u32[]{:S(2)}, u32[]{:S(2)}) collective-permute-start(bf16[128,2048]{1,0:T(8,128)(2,1)S(1)} %collective-permute-done), channel_id=1, source_target_pairs={{2,0},{4,2},{6,4},{8,6},{10,8},{12,10},{14,12},{16,14},{18,16},{20... | collective-permute-start | bytes 1572872 | tf_op jit(solution)/shard_map/ppermute | solution.py:14
  142.9 11.3 %collective-permute-start.2 = (bf16[128,2048]{1,0:T(8,128)(2,1)S(1)}, bf16[128,2048]{1,0:T(8,128)(2,1)S(1)}, u32[]{:S(2)}, u32[]{:S(2)}) collective-permute-start(bf16[128,2048]{1,0:T(8,128)(2,1)S(1)} %collective-permute-done.1), channel_id=1, source_target_pairs={{2,0},{4,2},{6,4},{8,6},{10,8},{12,10},{14,12},{16,14},{18,16},{20... | collective-permute-start | bytes 1572872 | tf_op jit(solution)/shard_map/ppermute | solution.py:14
  154.2 20.6 %collective-permute-start.3 = (bf16[128,2048]{1,0:T(8,128)(2,1)S(1)}, bf16[128,2048]{1,0:T(8,128)(2,1)S(1)}, u32[]{:S(2)}, u32[]{:S(2)}) collective-permute-start(bf16[128,2048]{1,0:T(8,128)(2,1)S(1)} %collective-permute-done.2), channel_id=1, source_target_pairs={{2,0},{4,2},{6,4},{8,6},{10,8},{12,10},{14,12},{16,14},{18,16},{20... | collective-permute-start | bytes 1572872 | tf_op jit(solution)/shard_map/ppermute | solution.py:14
  179.2 3.5 %copy-start = (f32[129,2048]{1,0:T(8,128)S(1)}, f32[129,2048]{1,0:T(8,128)}, u32[]{:S(2)}) copy-start(f32[129,2048]{1,0:T(8,128)} %get-tuple-element.31) | copy-start | bytes 3170308
  179.2 3.5 %copy-start.9 = (f32[2048]{0:T(1024)S(1)}, f32[2048]{0:T(1024)}, u32[]{:S(2)}) copy-start(f32[2048]{0:T(1024)} %param.7) | copy-start | bytes 24580
Sparse Core Ops, SparseCore 0:
  12.0 44.2 all-gather.1
  117.2 88.9 reduce-scatter.1
where the time goes:
time: 216 us; the launch traced here: 213 us
  waiting for transfers between devices  83.1 us (38%)
  matrix products  46.3 us (21%)
  other arithmetic  40.9 us (19%)
  starting transfers between devices  25.6 us (12%)
  between operations  14.3 us (7%)
  local copies, waits for them, and re-layouts  2.85 us (1%)
    ppermute x8, waiting for transfers between devices, passed_along(): return lax.ppermute(array, axis, pairs)  63.4 us
    ppermute x8, starting transfers between devices, passed_along(): return lax.ppermute(array, axis, pairs)  25.6 us
    dot_general x1, matrix products, body(): jnp.einsum('if,mfc->mic', inverse, products, precision=lax.Precision.HIGH...  23.8 us
    reduce_scatter x1, waiting for transfers between devices, body(): lax.psum_scatter(tap_terms, 'ctx', scatter_dimension=0, tiled=True)  19.6 us
    add x5, other arithmetic, times_conj(): first_real * second_real + first_imag * second_imag  15.2 us
    add x1, other arithmetic, body(): jnp.concatenate([pieces, empty], axis=0)  13.6 us
    dot_general x10, matrix products, spectrum(): jnp.dot(table, block.astype(jnp.float32), precision=lax.Precision.HIGHEST)  11.3 us
    dot_general x1, matrix products, body(): jnp.einsum('fr,mrc->mfc', table, filter_rows, precision=lax.Precision.HIG...  7.38 us
  transfers between devices with their start and end apart: 10, of which 9 were waited for; matrix products, arithmetic and copies ran while one was open for 15% of the time, Pallas kernels for 0%

commit v1 on v0

v1 whole, which is shorter than its diff:
```python
import functools

import jax
import jax.numpy as jnp
import numpy as np
from jax import lax
from jax.experimental import pallas as pl
from jax.experimental.pallas import tpu as pltpu
from jax.sharding import PartitionSpec as P

MESH = pl.DeviceIdType.MESH


def split_table(table):
    high = table.astype(jnp.bfloat16)
    low = (table - high.astype(np.float64)).astype(jnp.bfloat16)
    return np.concatenate([high, low], axis=1)


def tables(block):
    window = 2 * block
    odd = 2 * np.arange(block, dtype=np.int64)[:, None] + 1
    places = np.arange(window, dtype=np.int64)[None, :]
    angle = np.pi / window * (odd * places % (2 * window)).astype(np.float64)
    forward = np.concatenate([np.cos(angle), -np.sin(angle)], axis=0)
    inverse = forward[:, :block].T / block
    return split_table(forward), split_table(inverse)


def kernel(n, group, chunks, u_ref, g_ref, h_ref, fwd_hbm, inv_hbm, conv_ref, filt_ref,
           ubuf, gbuf, hbuf, cbuf, fbuf, fwd, inv, tsem, usem, gsem, hsem, osem, fsem,
           su, sg, sh, so, sf):
    me = lax.axis_index("ctx")
    place, layer = me % group, me // group
    layers = n // group
    own = hbuf.shape[2]
    width = own // chunks
    block = inv.shape[0]
    window = 2 * block

    def columns(q, c):
        return pl.ds(pl.multiple_of(q * own + c * width, 128), width)

    def whole(q):
        return pl.ds(pl.multiple_of(q * own, 128), own)

    def send(src, dst, send_sem, recv_sem, device):
        pltpu.make_async_remote_copy(
            src_ref=src, dst_ref=dst, send_sem=send_sem, recv_sem=recv_sem,
            device_id={"ctx": device}, device_id_type=MESH,
        ).start()

    def settle(ref, sem):
        pltpu.make_async_copy(ref, ref, sem).wait()

    barrier = pltpu.get_barrier_semaphore()

    def greet(d, carry):
        pl.semaphore_signal(barrier, inc=1, device_id={"ctx": (me + d) % n}, device_id_type=MESH)
        return carry

    lax.fori_loop(1, n, greet, 0)
    table_f = pltpu.make_async_copy(fwd_hbm, fwd, tsem.at[0])
    table_i = pltpu.make_async_copy(inv_hbm, inv, tsem.at[1])
    table_f.start()
    table_i.start()
    pltpu.make_async_copy(h_ref.at[:, whole(place)], hbuf.at[me], hsem).start()
    for c in range(chunks):
        pltpu.make_async_copy(u_ref.at[:, columns(place, c)], ubuf.at[c, place], usem.at[c]).start()
        pltpu.make_async_copy(g_ref.at[:, columns(place, c)], gbuf.at[c, 0, place], gsem.at[c, 0]).start()
    pl.semaphore_wait(barrier, n - 1)

    def send_taps(d, carry):
        other = (me + d) % n
        send(h_ref.at[:, whole(other % group)], hbuf.at[me], sh, hsem, other)
        return carry

    def send_grads_down(c):
        @pl.when(layer > 0)
        def _():
            for d in range(group):
                q = (place + d) % group
                send(g_ref.at[:, columns(q, c)], gbuf.at[c, 1, place], sg.at[c, 1], gsem.at[c, 1],
                     (layer - 1) * group + q)

    def send_in_layer(c):
        for d in range(1, group):
            q = (place + d) % group
            send(g_ref.at[:, columns(q, c)], gbuf.at[c, 0, place], sg.at[c, 0], gsem.at[c, 0],
                 layer * group + q)
        for d in range(1, group):
            q = (place + d) % group
            send(u_ref.at[:, columns(q, c)], ubuf.at[c, place], su.at[c], usem.at[c],
                 layer * group + q)

    send_grads_down(0)
    lax.fori_loop(1, n, send_taps, 0)
    send_in_layer(0)
    for c in range(1, chunks):
        send_grads_down(c)
        send_in_layer(c)

    def transform(x):
        rows = x.shape[0]
        return (jnp.dot(fwd[:, :rows], x, preferred_element_type=jnp.float32)
                + jnp.dot(fwd[:, window:window + rows], x, preferred_element_type=jnp.float32))

    def correlate(pairs):
        real, imag = 0.0, 0.0
        for first, second in pairs:
            ar, ai, br, bi = first[:block], first[block:], second[:block], second[block:]
            real = real + (ar * br + ai * bi)
            imag = imag + (ai * br - ar * bi)
        joined = jnp.concatenate([real, imag], axis=0)
        high = joined.astype(jnp.bfloat16)
        low = (joined - high.astype(jnp.float32)).astype(jnp.bfloat16)
        return (jnp.dot(inv[:, :window], high, preferred_element_type=jnp.float32)
                + jnp.dot(inv[:, window:], high, preferred_element_type=jnp.float32)
                + jnp.dot(inv[:, :window], low, preferred_element_type=jnp.float32))

    table_f.wait()
    table_i.wait()
    tokens = gbuf.shape[3]
    taps = group * tokens
    rows = hbuf.shape[1]

    def one_chunk(c, carry):
        settle(ubuf.at[c], usem.at[c])
        u = ubuf[c].reshape(taps, width)
        u_spec = [transform(u[b * block:(b + 1) * block]) for b in range(2)]
        settle(gbuf.at[c, 0], gsem.at[c, 0])

        @pl.when(layer < layers - 1)
        def _():
            settle(gbuf.at[c, 1], gsem.at[c, 1])

        @pl.when(layer == layers - 1)
        def _():
            gbuf[c, 1] = jnp.zeros(gbuf.shape[2:], jnp.bfloat16)

        g = gbuf[c].reshape(2 * taps, width)
        g_spec = [transform(g[b * block:b * block + window]) for b in range(3)]
        for m in range(2):
            part = correlate([(g_spec[b + m], u_spec[b]) for b in range(2)])
            fbuf[c, pl.ds(m * (n // 2), n // 2)] = part.reshape(n // 2, rows, width)

        def send_filter(d, inner):
            other = (me + d) % n
            send(fbuf.at[c, other], filt_ref.at[layer, :, columns(place, c)], sf.at[c], fsem, other)
            return inner

        lax.fori_loop(1, n, send_filter, 0)
        pltpu.make_async_copy(fbuf.at[c, me], filt_ref.at[layer, :, columns(place, c)], fsem).start()

        @pl.when(c == 0)
        def _():
            settle(hbuf, hsem)

        h = hbuf[:, :, pl.ds(pl.multiple_of(c * width, 128), width)].astype(jnp.float32)
        h = h.reshape(taps, width).astype(jnp.bfloat16)
        h_spec = [transform(h[b * block:(b + 1) * block]) for b in range(2)]
        for s in range(2):
            part = correlate([(g_spec[s + m], h_spec[m]) for m in range(2)])
            cbuf[c, pl.ds(s * (group // 2), group // 2)] = part.reshape(group // 2, tokens, width)
        for d in range(1, group):
            q = (place + d) % group
            send(cbuf.at[c, q], conv_ref.at[:, columns(place, c)], so.at[c], osem, layer * group + q)
        pltpu.make_async_copy(cbuf.at[c, place], conv_ref.at[:, columns(place, c)], osem).start()
        return carry

    lax.fori_loop(0, chunks, one_chunk, 0)

    settle(conv_ref, osem)
    settle(filt_ref, fsem)
    settle(hbuf.at[pl.ds(0, n - 1)], sh)
    for c in range(chunks):
        settle(ubuf.at[c, pl.ds(0, group - 1)], su.at[c])
        settle(gbuf.at[c, 0, pl.ds(0, group - 1)], sg.at[c, 0])
        settle(cbuf.at[c, pl.ds(0, group - 1)], so.at[c])
        settle(fbuf.at[c, pl.ds(0, n - 1)], sf.at[c])

        @pl.when(layer > 0)
        def _():
            settle(gbuf.at[c, 1], sg.at[c, 1])


def body(n, inputs, out_grad, filter_taps, skip_gain):
    tokens, columns = inputs.shape
    rows = filter_taps.shape[0]
    taps = rows * n
    group = taps // tokens
    own = columns // group
    chunks = 2 if own % 256 == 0 else 1
    width = own // chunks
    block = taps // 2
    forward, inverse = tables(block)
    bf16, f32 = jnp.bfloat16, jnp.float32
    anywhere = pl.BlockSpec(memory_space=pl.ANY)
    dma = pltpu.SemaphoreType.DMA
    conv, filt = pl.pallas_call(
        functools.partial(kernel, n, group, chunks),
        out_shape=(
            jax.ShapeDtypeStruct((tokens, columns), f32),
            jax.ShapeDtypeStruct((n // group, rows, columns), f32),
        ),
        in_specs=[anywhere] * 5,
        out_specs=(anywhere, anywhere),
        scratch_shapes=[
            pltpu.VMEM((chunks, group, tokens, width), bf16),
            pltpu.VMEM((chunks, 2, group, tokens, width), bf16),
            pltpu.VMEM((n, rows, own), bf16),
            pltpu.VMEM((chunks, group, tokens, width), f32),
            pltpu.VMEM((chunks, n, rows, width), f32),
            pltpu.VMEM(forward.shape, bf16),
            pltpu.VMEM(inverse.shape, bf16),
            dma((2,)),
            dma((chunks,)),
            dma((chunks, 2)),
            dma,
            dma,
            dma,
            dma((chunks,)),
            dma((chunks, 2)),
            dma,
            dma((chunks,)),
            dma((chunks,)),
        ],
        compiler_params=pltpu.CompilerParams(
            collective_id=0, has_side_effects=True, vmem_limit_bytes=40 * 1024 * 1024
        ),
        cost_estimate=pl.CostEstimate(
            flops=2 * 5 * taps * taps * own * 4, bytes_accessed=8 * tokens * columns, transcendentals=0
        ),
        name="spectral_exchange",
    )(inputs, out_grad, filter_taps, jnp.asarray(forward), jnp.asarray(inverse))
    input_grad = skip_gain[None, :] * out_grad.astype(f32) + conv
    return input_grad, jnp.sum(filt, axis=0)


def solution(mesh):
    in_specs = (P("ctx", "ch"), P("ctx", "ch"), P("ctx", "ch"), P("ch"))
    out_specs = (P("ctx", "ch"), P("ctx", "ch"))
    return jax.shard_map(functools.partial(body, mesh.shape["ctx"]), mesh=mesh,
                         in_specs=in_specs, out_specs=out_specs, check_vma=False)
```

time: 216 us -> 60.2 us (0.28); the launches traced: 213 us -> 59.9 us
  waiting for transfers between devices: 83.1 us -> 0 us
  Pallas kernels: 0 us -> 52.1 us
  matrix products: 46.3 us -> 0 us
  other arithmetic: 40.9 us -> 1.89 us
  starting transfers between devices: 25.6 us -> 0 us
  between operations: 14.3 us -> 0.66 us
  local copies, waits for them, and re-layouts: 2.85 us -> 5.25 us
    ppermute x8 -> x0, waiting for transfers between devices: 63.4 us -> none  [passed_along(): return lax.ppermute(array, axis, pairs)]
    pallas_call x0 -> x1, Pallas kernels: none -> 52.1 us  [body(): pl.pallas_call(functools.partial(kernel, n, group, chunks), out_shape=(ja...]
    dot_general x13 -> x0, matrix products: 46.3 us -> none  [the longest x1 23.8 us: body(): jnp.einsum('if,mfc->mic', inverse, products, precision=lax.Precision.HIGH...]
    add x7 -> x1, other arithmetic: 31.6 us -> 1.12 us  [body(): input_grad = skip_gain[None, :] * out_grad.astype(f32) + conv]
    ppermute x8 -> x0, starting transfers between devices: 25.6 us -> none  [passed_along(): return lax.ppermute(array, axis, pairs)]
    reduce_scatter x1 -> x0, waiting for transfers between devices: 19.6 us -> none  [body(): lax.psum_scatter(tap_terms, 'ctx', scatter_dimension=0, tiled=True)]
    unnamed x4 -> x0, other arithmetic: 6.11 us -> none
    unnamed x20 -> x12, local copies, waits for them, and re-layouts: 2.76 us -> 5.25 us
  transfers between devices with their start and end apart: 10 -> 0, of which waited for: 9 -> 0; matrix products, arithmetic and copies ran while one was open for 15% -> 0% of each run, Pallas kernels for 0% -> 0%
where the time goes in v1:
time: 60.2 us; the launch traced here: 59.9 us
  Pallas kernels  52.1 us (87%)
  local copies, waits for them, and re-layouts  5.25 us (9%)
  other arithmetic  1.89 us (3%)
  between operations  0.66 us (1%)
    pallas_call x1, Pallas kernels, body(): pl.pallas_call(functools.partial(kernel, n, group, chunks), out_shape=(ja...  52.1 us
    unnamed x12, local copies, waits for them, and re-layouts  5.25 us

profile of v1, /device:TPU:1, one launch (start us, length us, event | category | flops | bytes accessed | tf_op | source)
XLA Modules:
  0.0 59.9 jit_solution(1170998189425406417)
XLA Ops:
  0.6 0.0 copy-start
  0.6 1.0 %copy-done = bf16[128,2048]{1,0:T(8,128)(2,1)S(1)} copy-done((bf16[128,2048]{1,0:T(8,128)(2,1)S(1)}, bf16[128,2048]{1,0:T(8,128)(2,1)}, u32[]{:S(2)}) %copy-start) | copy-done | bytes 524312
  1.7 0.0 copy-start.1
  1.7 1.0 %copy-done.1 = bf16[128,2048]{1,0:T(8,128)(2,1)S(1)} copy-done((bf16[128,2048]{1,0:T(8,128)(2,1)S(1)}, bf16[128,2048]{1,0:T(8,128)(2,1)}, u32[]{:S(2)}) %copy-start.1) | copy-done | bytes 524312
  2.7 0.0 copy-start.2
  2.7 0.9 %copy-done.2 = bf16[32,2048]{1,0:T(8,128)(2,1)S(1)} copy-done((bf16[32,2048]{1,0:T(8,128)(2,1)S(1)}, bf16[32,2048]{1,0:T(8,128)(2,1)}, u32[]{:S(2)}) %copy-start.2) | copy-done | bytes 131096
  3.6 0.0 copy-start.3
  3.6 1.2 %copy-done.3 = bf16[512,1024]{1,0:T(8,128)(2,1)S(1)} copy-done((bf16[512,1024]{1,0:T(8,128)(2,1)S(1)}, bf16[512,1024]{1,0:T(8,128)(2,1)}, u32[]{:S(2)}) %copy-start.3) | copy-done | bytes 1048600
  4.8 0.0 copy-start.4
  4.8 1.0 %copy-done.4 = bf16[256,1024]{1,0:T(8,128)(2,1)S(1)} copy-done((bf16[256,1024]{1,0:T(8,128)(2,1)S(1)}, bf16[256,1024]{1,0:T(8,128)(2,1)}, u32[]{:S(2)}) %copy-start.4) | copy-done | bytes 524312
  5.9 0.0 copy-start.5
  5.9 52.1 %spectral_exchange.1 = (f32[128,2048]{1,0:T(8,128)S(1)}, f32[4,32,2048]{2,1,0:T(8,128)S(1)}) custom-call(bf16[128,2048]{1,0:T(8,128)(2,1)S(1)} %copy-done.1, bf16[128,2048]{1,0:T(8,128)(2,1)S(1)} %copy-done, bf16[32,2048]{1,0:T(8,128)(2,1)S(1)} %copy-done.2, bf16[512,1024]{1,0:T(8,128)(2,1)S(1)} %copy-done.3, bf16[256,1024]{1,0:T(8,128)(2,1)S(1)} %copy-done.4), custom_call_target="tpu_custom_call" | custom-call | flops 5368709120 | bytes 2097152 | tf_op jit(solution)/shard_map/spectral_exchange/pallas_call | solution.py:200
  58.0 0.0 copy-done.5
  58.0 1.1 %multiply_add_fusion = f32[128,2048]{1,0:T(8,128)} fusion(f32[128,2048]{1,0:T(8,128)S(1)} %get-tuple-element.4, bf16[128,2048]{1,0:T(8,128)(2,1)S(1)} %copy-done, f32[2048]{0:T(1024)S(1)} %copy-done.5), kind=kLoop, calls=%fused_computation | loop fusion | flops 786432 | bytes 2629632 | tf_op jit(solution)/shard_map/add | solution.py:236
  59.1 0.8 %reduce_sum.9 = f32[32,2048]{1,0:T(8,128)} reduce(f32[4,32,2048]{2,1,0:T(8,128)S(1)} %get-tuple-element.5, f32[]{:T(128)} %constant.2.clone.1), dimensions={0}, to_apply=%region_0.0 | reduce | flops 196608 | bytes 1310724 | tf_op jit(solution)/shard_map/reduce_sum | solution.py:237
Async XLA Ops:
  0.6 1.0 %copy-start = (bf16[128,2048]{1,0:T(8,128)(2,1)S(1)}, bf16[128,2048]{1,0:T(8,128)(2,1)}, u32[]{:S(2)}) copy-start(bf16[128,2048]{1,0:T(8,128)(2,1)} %g_ref.1) | copy-start | bytes 1572868
  1.7 1.0 %copy-start.1 = (bf16[128,2048]{1,0:T(8,128)(2,1)S(1)}, bf16[128,2048]{1,0:T(8,128)(2,1)}, u32[]{:S(2)}) copy-start(bf16[128,2048]{1,0:T(8,128)(2,1)} %u_ref.1) | copy-start | bytes 1572868
  2.7 0.9 %copy-start.2 = (bf16[32,2048]{1,0:T(8,128)(2,1)S(1)}, bf16[32,2048]{1,0:T(8,128)(2,1)}, u32[]{:S(2)}) copy-start(bf16[32,2048]{1,0:T(8,128)(2,1)} %h_ref.1) | copy-start | bytes 393220
  3.6 1.2 %copy-start.3 = (bf16[512,1024]{1,0:T(8,128)(2,1)S(1)}, bf16[512,1024]{1,0:T(8,128)(2,1)}, u32[]{:S(2)}) copy-start(bf16[512,1024]{1,0:T(8,128)(2,1)} %constant.6.clone.fwd_hbm) | copy-start | bytes 3145732
  4.8 1.0 %copy-start.4 = (bf16[256,1024]{1,0:T(8,128)(2,1)S(1)}, bf16[256,1024]{1,0:T(8,128)(2,1)}, u32[]{:S(2)}) copy-start(bf16[256,1024]{1,0:T(8,128)(2,1)} %constant.7.clone.inv_hbm) | copy-start | bytes 1572868
  5.9 52.1 %copy-start.5 = (f32[2048]{0:T(1024)S(1)}, f32[2048]{0:T(1024)}, u32[]{:S(2)}) copy-start(f32[2048]{0:T(1024)} %param.9) | copy-start | bytes 24580

commit v2 on v1

--- a/solution.py
+++ b/solution.py
@@ -28,12 +28,13 @@
 
 
 def kernel(n, group, chunks, u_ref, g_ref, h_ref, fwd_hbm, inv_hbm, conv_ref, filt_ref,
-           ubuf, gbuf, hbuf, cbuf, fbuf, fwd, inv, tsem, usem, gsem, hsem, osem, fsem,
-           su, sg, sh, so, sf):
+           ubuf, gbuf, hbuf, cbuf, fbuf, fwd, inv, tsem, usem, gsem, halo, hsem, osem, fsem,
+           su, sg, st, sh, so, sf):
     me = lax.axis_index("ctx")
     place, layer = me % group, me // group
-    layers = n // group
-    own = hbuf.shape[2]
+    layers, pairs = n // group, group // 2
+    pair, core = place // 2, place % 2
+    own = hbuf.shape[3]
     width = own // chunks
     block = inv.shape[0]
     window = 2 * block
@@ -64,41 +65,101 @@
     table_i = pltpu.make_async_copy(inv_hbm, inv, tsem.at[1])
     table_f.start()
     table_i.start()
-    pltpu.make_async_copy(h_ref.at[:, whole(place)], hbuf.at[me], hsem).start()
-    for c in range(chunks):
+    pltpu.make_async_copy(h_ref.at[:, whole(place)], hbuf.at[layer, place], hsem.at[layer]).start()
+    for c in range(chunks):
+        pltpu.make_async_copy(g_ref.at[:, columns(place, c)], gbuf.at[c, 0, pair, core], gsem.at[c, pair]).start()
         pltpu.make_async_copy(u_ref.at[:, columns(place, c)], ubuf.at[c, place], usem.at[c]).start()
-        pltpu.make_async_copy(g_ref.at[:, columns(place, c)], gbuf.at[c, 0, place], gsem.at[c, 0]).start()
     pl.semaphore_wait(barrier, n - 1)
-
-    def send_taps(d, carry):
-        other = (me + d) % n
-        send(h_ref.at[:, whole(other % group)], hbuf.at[me], sh, hsem, other)
-        return carry
 
     def send_grads_down(c):
         @pl.when(layer > 0)
         def _():
-            for d in range(group):
-                q = (place + d) % group
-                send(g_ref.at[:, columns(q, c)], gbuf.at[c, 1, place], sg.at[c, 1], gsem.at[c, 1],
+            for e in range(2):
+                q = pair * 2 + (core + e) % 2
+                send(g_ref.at[:, columns(q, c)], gbuf.at[c, 1, pair, core], sg.at[c, 1], halo.at[c],
                      (layer - 1) * group + q)
 
-    def send_in_layer(c):
+    def send_grads(c):
         for d in range(1, group):
-            q = (place + d) % group
-            send(g_ref.at[:, columns(q, c)], gbuf.at[c, 0, place], sg.at[c, 0], gsem.at[c, 0],
+            q = (place + group - d) % group
+            send(g_ref.at[:, columns(q, c)], gbuf.at[c, 0, pair, core], sg.at[c, 0], gsem.at[c, pair],
                  layer * group + q)
+
+    def send_inputs(c):
         for d in range(1, group):
             q = (place + d) % group
             send(u_ref.at[:, columns(q, c)], ubuf.at[c, place], su.at[c], usem.at[c],
                  layer * group + q)
 
-    send_grads_down(0)
-    lax.fori_loop(1, n, send_taps, 0)
-    send_in_layer(0)
-    for c in range(1, chunks):
+    def forward_grads(c):
+        for d in range(1, pairs):
+            other = (pair + d) % pairs
+            settle(gbuf.at[c, 0, other], gsem.at[c, other])
+
+            @pl.when(layer > 0)
+            def _():
+                send(gbuf.at[c, 0, other], gbuf.at[c, 1, other], sg.at[c, 1], halo.at[c], me - group)
+
+    def pass_taps(slot, way, step):
+        send(hbuf.at[slot], hbuf.at[slot], sh.at[way, step], hsem.at[slot], me + (1 - 2 * way) * group)
+
+    for d in range(1, group):
+        q = (place + d) % group
+        send(h_ref.at[:, whole(q)], hbuf.at[layer, place], st, hsem.at[layer], layer * group + q)
+    for c in range(chunks):
         send_grads_down(c)
-        send_in_layer(c)
+        send_grads(c)
+    for c in range(chunks):
+        send_inputs(c)
+    settle(hbuf.at[layer], hsem.at[layer])
+
+    @pl.when(layer > 0)
+    def _():
+        pass_taps(layer, 1, 0)
+
+    @pl.when(layer < layers - 1)
+    def _():
+        pass_taps(layer, 0, 0)
+
+    for c in range(chunks):
+        forward_grads(c)
+
+    def forward_taps(step, carry):
+        @pl.when((layer >= step) & (layer < layers - 1))
+        def _():
+            settle(hbuf.at[layer - step], hsem.at[layer - step])
+            pass_taps(layer - step, 0, step)
+
+        @pl.when((layer + step < layers) & (layer > 0))
+        def _():
+            settle(hbuf.at[layer + step], hsem.at[layer + step])
+            pass_taps(layer + step, 1, step)
+
+        return carry
+
+    lax.fori_loop(1, layers, forward_taps, 0)
+
+    def last_taps(step, carry):
+        @pl.when(layer == layers - 1)
+        def _():
+            settle(hbuf.at[layers - 1 - step], hsem.at[layers - 1 - step])
+
+        @pl.when(layer == 0)
+        def _():
+            settle(hbuf.at[step], hsem.at[step])
+
+        return carry
+
+    def sent_taps(step, carry):
+        @pl.when((layer >= step) & (layer < layers - 1))
+        def _():
+            settle(hbuf.at[0], sh.at[0, step])
+
+        @pl.when((layer + step < layers) & (layer > 0))
+        def _():
+            settle(hbuf.at[0], sh.at[1, step])
+
+        return carry
 
     def transform(x):
         rows = x.shape[0]
@@ -120,19 +181,19 @@
 
     table_f.wait()
     table_i.wait()
-    tokens = gbuf.shape[3]
+    tokens = ubuf.shape[2]
     taps = group * tokens
-    rows = hbuf.shape[1]
+    rows = hbuf.shape[2]
 
     def one_chunk(c, carry):
         settle(ubuf.at[c], usem.at[c])
         u = ubuf[c].reshape(taps, width)
         u_spec = [transform(u[b * block:(b + 1) * block]) for b in range(2)]
-        settle(gbuf.at[c, 0], gsem.at[c, 0])
+        settle(gbuf.at[c, 0, pair], gsem.at[c, pair])
 
         @pl.when(layer < layers - 1)
         def _():
-            settle(gbuf.at[c, 1], gsem.at[c, 1])
+            settle(gbuf.at[c, 1], halo.at[c])
 
         @pl.when(layer == layers - 1)
         def _():
@@ -154,9 +215,9 @@
 
         @pl.when(c == 0)
         def _():
-            settle(hbuf, hsem)
-
-        h = hbuf[:, :, pl.ds(pl.multiple_of(c * width, 128), width)].astype(jnp.float32)
+            lax.fori_loop(1, layers, last_taps, 0)
+
+        h = hbuf[:, :, :, pl.ds(pl.multiple_of(c * width, 128), width)].astype(jnp.float32)
         h = h.reshape(taps, width).astype(jnp.bfloat16)
         h_spec = [transform(h[b * block:(b + 1) * block]) for b in range(2)]
         for s in range(2):
@@ -172,10 +233,11 @@
 
     settle(conv_ref, osem)
     settle(filt_ref, fsem)
-    settle(hbuf.at[pl.ds(0, n - 1)], sh)
+    settle(hbuf.at[0, pl.ds(0, group - 1)], st)
+    lax.fori_loop(0, layers, sent_taps, 0)
     for c in range(chunks):
         settle(ubuf.at[c, pl.ds(0, group - 1)], su.at[c])
-        settle(gbuf.at[c, 0, pl.ds(0, group - 1)], sg.at[c, 0])
+        settle(ubuf.at[c, pl.ds(0, group - 1)], sg.at[c, 0])
         settle(cbuf.at[c, pl.ds(0, group - 1)], so.at[c])
         settle(fbuf.at[c, pl.ds(0, n - 1)], sf.at[c])
 
@@ -203,30 +265,32 @@
             jax.ShapeDtypeStruct((tokens, columns), f32),
             jax.ShapeDtypeStruct((n // group, rows, columns), f32),
         ),
-        in_specs=[anywhere] * 5,
+        in_specs=[pl.BlockSpec(memory_space=pltpu.HBM)] * 5,
         out_specs=(anywhere, anywhere),
         scratch_shapes=[
             pltpu.VMEM((chunks, group, tokens, width), bf16),
-            pltpu.VMEM((chunks, 2, group, tokens, width), bf16),
-            pltpu.VMEM((n, rows, own), bf16),
+            pltpu.VMEM((chunks, 2, group // 2, 2, tokens, width), bf16),
+            pltpu.VMEM((n // group, group, rows, own), bf16),
             pltpu.VMEM((chunks, group, tokens, width), f32),
             pltpu.VMEM((chunks, n, rows, width), f32),
             pltpu.VMEM(forward.shape, bf16),
             pltpu.VMEM(inverse.shape, bf16),
             dma((2,)),
             dma((chunks,)),
+            dma((chunks, group // 2)),
+            dma((chunks,)),
+            dma((n // group,)),
+            dma,
+            dma,
+            dma((chunks,)),
             dma((chunks, 2)),
             dma,
-            dma,
-            dma,
-            dma((chunks,)),
-            dma((chunks, 2)),
-            dma,
+            dma((2, n // group)),
             dma((chunks,)),
             dma((chunks,)),
         ],
         compiler_params=pltpu.CompilerParams(
-            collective_id=0, has_side_effects=True, vmem_limit_bytes=40 * 1024 * 1024
+            collective_id=0, has_side_effects=True, vmem_limit_bytes=63 * 1024 * 1024
         ),
         cost_estimate=pl.CostEstimate(
             flops=2 * 5 * taps * taps * own * 4, bytes_accessed=8 * tokens * columns, transcendentals=0

time: 60.2 us -> 59.9 us (level)
  local copies, waits for them, and re-layouts: 5.25 us -> 0.01 us
  Pallas kernels: 52.1 us -> 55.9 us
  other arithmetic: 1.89 us -> 3.19 us
    unnamed x12 -> x6, local copies, waits for them, and re-layouts: 5.25 us -> 0.01 us
    pallas_call x1, Pallas kernels: 52.1 us -> 55.9 us  [body(): pl.pallas_call(functools.partial(kernel, n, group, chunks), out_shape=(ja...]
    add x1, other arithmetic: 1.12 us -> 2.42 us  [body(): input_grad = skip_gain[None, :] * out_grad.astype(f32) + conv]
where the time goes in v2:
time: 59.9 us; the launch traced here: 59.8 us
  Pallas kernels  55.9 us (93%)
  other arithmetic  3.19 us (5%)
  between operations  0.68 us (1%)
    pallas_call x1, Pallas kernels, body(): pl.pallas_call(functools.partial(kernel, n, group, chunks), out_shape=(ja...  55.9 us
    add x1, other arithmetic, body(): input_grad = skip_gain[None, :] * out_grad.astype(f32) + conv  2.42 us

profile of v2, /device:TPU:1, one launch (start us, length us, event | category | flops | bytes accessed | tf_op | source)
XLA Modules:
  0.0 59.8 jit_solution(16760115379039607357)
XLA Ops:
  0.6 0.0 copy-start.1
  0.6 0.0 copy-start.2
  0.7 55.9 %spectral_exchange.1 = (f32[128,2048]{1,0:T(8,128)}, f32[4,32,2048]{2,1,0:T(8,128)}) custom-call(bf16[128,2048]{1,0:T(8,128)(2,1)} %u_ref.1, bf16[128,2048]{1,0:T(8,128)(2,1)} %g_ref.1, bf16[32,2048]{1,0:T(8,128)(2,1)} %h_ref.1, bf16[512,1024]{1,0:T(8,128)(2,1)} %constant.6.clone.fwd_hbm, bf16[256,1024]{1,0:T(8,128)(2,1)} %constant.7.clone.inv_hbm), custom_call_target="tpu_custom_call" | custom-call | flops 5368709120 | bytes 2097152 | tf_op jit(solution)/shard_map/spectral_exchange/pallas_call | solution.py:262
  56.5 0.0 copy-done.1
  56.5 0.0 copy-done.2
  56.6 0.0 copy-start
  56.6 2.4 %multiply_add_fusion = f32[128,2048]{1,0:T(8,128)} fusion(f32[128,2048]{1,0:T(8,128)} %get-tuple-element.4, bf16[128,2048]{1,0:T(8,128)(2,1)S(1)} %copy-done.1, f32[2048]{0:T(1024)S(1)} %copy-done.2), kind=kLoop, calls=%fused_computation | loop fusion | flops 786432 | bytes 2629632 | tf_op jit(solution)/shard_map/add | solution.py:300
  59.0 0.0 copy-done
  59.0 0.8 %reduce_sum.9 = f32[32,2048]{1,0:T(8,128)} reduce(f32[4,32,2048]{2,1,0:T(8,128)S(1)} %copy-done, f32[]{:T(128)} %constant.2.clone.1), dimensions={0}, to_apply=%region_0.0 | reduce | flops 196608 | bytes 1310724 | tf_op jit(solution)/shard_map/reduce_sum | solution.py:301
Async XLA Ops:
  0.6 55.9 %copy-start.1 = (bf16[128,2048]{1,0:T(8,128)(2,1)S(1)}, bf16[128,2048]{1,0:T(8,128)(2,1)}, u32[]{:S(2)}) copy-start(bf16[128,2048]{1,0:T(8,128)(2,1)} %g_ref.1) | copy-start | bytes 1572868
  0.6 55.9 %copy-start.2 = (f32[2048]{0:T(1024)S(1)}, f32[2048]{0:T(1024)}, u32[]{:S(2)}) copy-start(f32[2048]{0:T(1024)} %param.9) | copy-start | bytes 24580
  56.6 2.4 %copy-start = (f32[4,32,2048]{2,1,0:T(8,128)S(1)}, f32[4,32,2048]{2,1,0:T(8,128)}, u32[]{:S(2)}) copy-start(f32[4,32,2048]{2,1,0:T(8,128)} %get-tuple-element.5) | copy-start | bytes 3145732
